TPU v7x, 32 devices: a whole 2x2x4 slice. The times are simulated.
32 devices in a mesh: dp: 32 (over z, y, x, core).
Axes of the slice: x: 2, y: 2, z: 4, core: 2. Of those that a mesh axis runs over, the one named last changes fastest.
Arguments:
- tokens: bfloat16 [32768, 768], P('dp'), may hold values from -6 to 6
- segment: int32 [32768], P('dp'), may hold values from -1 to 4, as said below
- ln1_gain: bfloat16 [768], P('dp'), may hold values from 0.099609375 to 1.8984375
- ln1_bias: bfloat16 [768], P('dp'), may hold values from -3 to 3
- w_qkv: bfloat16 [768, 2304], P('dp'), may hold values from -0.21875 to 0.21875
- b_query: bfloat16 [768], P('dp'), may hold values from -3 to 3
- b_value: bfloat16 [768], P('dp'), may hold values from -3 to 3
- w_out: bfloat16 [768, 768], P('dp'), may hold values from -3.5 to 3.5
- b_out: bfloat16 [768], P('dp'), may hold values from -3 to 3
- ln2_gain: bfloat16 [768], P('dp'), may hold values from 0.099609375 to 1.8984375
- ln2_bias: bfloat16 [768], P('dp'), may hold values from -3 to 3
- w_up: bfloat16 [768, 3072], P('dp'), may hold values from -0.21875 to 0.21875
- b_up: bfloat16 [3072], P('dp'), may hold values from -3 to 3
- w_down: bfloat16 [3072, 768], P('dp'), may hold values from -0.109375 to 0.109375
- b_down: bfloat16 [768], P('dp'), may hold values from -3 to 3
- cotangent: bfloat16 [32768, 768], P('dp'), may hold values from -6 to 6
Outputs:
- block_out: bfloat16 [32768, 768], P('dp')
- grad_tokens: bfloat16 [32768, 768], P('dp')
- grad_ln1_gain: float32 [768], P('dp')
- grad_ln1_bias: float32 [768], P('dp')
- grad_w_qkv: float32 [768, 2304], P('dp')
- grad_b_query: float32 [768], P('dp')
- grad_b_value: float32 [768], P('dp')
- grad_w_out: float32 [768, 768], P('dp')
- grad_b_out: float32 [768], P('dp')
- grad_ln2_gain: float32 [768], P('dp')
- grad_ln2_bias: float32 [768], P('dp')
- grad_w_up: float32 [768, 3072], P('dp')
- grad_b_up: float32 [3072], P('dp')
- grad_w_down: float32 [3072, 768], P('dp')
- grad_b_down: float32 [768], P('dp')
Inputs may be any that keep to these rules, and one draw needn't show every extreme that they name: `segment`: each device's 1024 rows hold whole sequences, each of 196 rows (a clip) or 314 rows (a video), labelled 0, 1, 2, ... in row order, then -1 on the rows left over; no sequence crosses devices.
All inputs are finite; a program needn't handle non-finite values.
Results may differ from a plain program's by a relative error of at most 0.012.
Values may be sent and summed in bfloat16 or wider, within the bound.
No kernel may reach another device: no remote copies, remote signals or barrier semaphores. Data moves between devices by JAX's collectives and lax.ppermute only.
A program may use at most 192 MiB of HBM per device.

v0:
```python
import jax
import jax.numpy as jnp
from jax import lax
from jax.sharding import PartitionSpec as P

HEADS = 12


EPSILON = 1e-06
NEGATIVE = -1000000000.0


def layer_norm(values, scale_gain, offset):
    center = values - jnp.mean(values, -1, keepdims=True)
    spread = jnp.mean(center * center, -1, keepdims=True)
    inverse = lax.rsqrt(spread + EPSILON)
    normal = center * inverse
    return (normal * scale_gain + offset, normal, inverse)


def norm_back(grad_result, normal, inverse, scale_gain):
    grad_normal = grad_result * scale_gain
    part_one = jnp.mean(grad_normal, -1, keepdims=True)
    part_two = jnp.mean(grad_normal * normal, -1, keepdims=True)
    grad_values = inverse * (grad_normal - part_one - normal * part_two)
    return (grad_values, jnp.sum(grad_result * normal, 0), jnp.sum(grad_result, 0))


def masked_scores(query_head, key_head, same_seq, score_scale):
    scores = jnp.dot(query_head, key_head.T, preferred_element_type=jnp.float32) * score_scale
    return jnp.where(same_seq, scores, NEGATIVE)


def local(
    tokens,
    segment,
    ln1_gain,
    ln1_bias,
    w_qkv,
    b_query,
    b_value,
    w_out,
    b_out,
    ln2_gain,
    ln2_bias,
    w_up,
    b_up,
    w_down,
    b_down,
    cotangent,
):
    shards = (
        ln1_gain,
        ln1_bias,
        w_qkv,
        b_query,
        b_value,
        w_out,
        b_out,
        ln2_gain,
        ln2_bias,
        w_up,
        b_up,
        w_down,
        b_down,
    )
    gathered = (
        lax.all_gather(shards[0], "dp", axis=0, tiled=True),
        lax.all_gather(shards[1], "dp", axis=0, tiled=True),
        lax.all_gather(shards[2], "dp", axis=0, tiled=True),
        lax.all_gather(shards[3], "dp", axis=0, tiled=True),
        lax.all_gather(shards[4], "dp", axis=0, tiled=True),
        lax.all_gather(shards[5], "dp", axis=0, tiled=True),
        lax.all_gather(shards[6], "dp", axis=0, tiled=True),
        lax.all_gather(shards[7], "dp", axis=0, tiled=True),
        lax.all_gather(shards[8], "dp", axis=0, tiled=True),
        lax.all_gather(shards[9], "dp", axis=0, tiled=True),
        lax.all_gather(shards[10], "dp", axis=0, tiled=True),
        lax.all_gather(shards[11], "dp", axis=0, tiled=True),
        lax.all_gather(shards[12], "dp", axis=0, tiled=True),
    )
    (
        gain_one,
        bias_one,
        qkv_full,
        query_bias,
        value_bias,
        out_full,
        out_bias,
        gain_two,
        bias_two,
        up_full,
        up_bias,
        down_full,
        down_bias,
    ) = gathered
    row_count, model_width = tokens.shape
    head_dim = model_width // HEADS
    score_scale = head_dim ** (-0.5)
    inputs = tokens.astype(jnp.float32)
    keep_rows = (segment >= 0).astype(jnp.float32)[:, None]
    same_seq = segment[:, None] == segment[None, :]

    def split_heads(matrix):
        return matrix.reshape(row_count, HEADS, head_dim).transpose(1, 0, 2)

    def join_heads(stacked):
        return stacked.transpose(1, 0, 2).reshape(row_count, model_width)

    normed, normal_one, inverse_one = layer_norm(
        inputs, gain_one.astype(jnp.float32), bias_one.astype(jnp.float32)
    )
    normed_low = normed.astype(jnp.bfloat16)
    packed = jnp.dot(normed_low, qkv_full, preferred_element_type=jnp.float32)
    query_rows = (packed[:, :model_width] + query_bias.astype(jnp.float32)).astype(jnp.bfloat16)
    key_rows = packed[:, model_width : 2 * model_width].astype(jnp.bfloat16)
    value_rows = (packed[:, 2 * model_width :] + value_bias.astype(jnp.float32)).astype(
        jnp.bfloat16
    )
    query_heads = split_heads(query_rows)
    key_heads = split_heads(key_rows)
    value_heads = split_heads(value_rows)

    def head_forward(head_item):
        query_head, key_head, value_head = head_item
        scores = masked_scores(query_head, key_head, same_seq, score_scale)
        row_max = jnp.max(scores, -1, keepdims=True)
        exponent = jnp.exp(scores - row_max)
        row_total = jnp.sum(exponent, -1, keepdims=True)
        softmax_rows = (exponent / row_total).astype(jnp.bfloat16)
        mixed_head = jnp.dot(softmax_rows, value_head, preferred_element_type=jnp.float32)
        return (mixed_head, row_max + jnp.log(row_total))

    mixed_heads, log_total = lax.map(head_forward, (query_heads, key_heads, value_heads))
    mixed_rows = join_heads(mixed_heads).astype(jnp.bfloat16)
    branch = jnp.dot(mixed_rows, out_full, preferred_element_type=jnp.float32) + out_bias.astype(
        jnp.float32
    )
    middle = inputs + keep_rows * branch
    normed_two, normal_two, inverse_two = layer_norm(
        middle, gain_two.astype(jnp.float32), bias_two.astype(jnp.float32)
    )
    normed_two_low = normed_two.astype(jnp.bfloat16)
    hidden = jnp.dot(normed_two_low, up_full, preferred_element_type=jnp.float32) + up_bias.astype(
        jnp.float32
    )
    active = jax.nn.gelu(hidden).astype(jnp.bfloat16)
    result = middle + keep_rows * (
        jnp.dot(active, down_full, preferred_element_type=jnp.float32)
        + down_bias.astype(jnp.float32)
    )
    regathered = (
        lax.all_gather(shards[0], "dp", axis=0, tiled=True),
        lax.all_gather(shards[1], "dp", axis=0, tiled=True),
        lax.all_gather(shards[2], "dp", axis=0, tiled=True),
        lax.all_gather(shards[3], "dp", axis=0, tiled=True),
        lax.all_gather(shards[4], "dp", axis=0, tiled=True),
        lax.all_gather(shards[5], "dp", axis=0, tiled=True),
        lax.all_gather(shards[6], "dp", axis=0, tiled=True),
        lax.all_gather(shards[7], "dp", axis=0, tiled=True),
        lax.all_gather(shards[8], "dp", axis=0, tiled=True),
        lax.all_gather(shards[9], "dp", axis=0, tiled=True),
        lax.all_gather(shards[10], "dp", axis=0, tiled=True),
        lax.all_gather(shards[11], "dp", axis=0, tiled=True),
        lax.all_gather(shards[12], "dp", axis=0, tiled=True),
    )
    gain_one_back, qkv_back, out_back = (regathered[0], regathered[2], regathered[5])
    gain_two_back, up_back, down_back = (regathered[7], regathered[9], regathered[11])
    grad_result = cotangent.astype(jnp.float32)
    grad_branch_two = (keep_rows * grad_result).astype(jnp.bfloat16)
    grad_down = jnp.dot(active.T, grad_branch_two, preferred_element_type=jnp.float32)
    grad_down_bias = jnp.sum(grad_branch_two.astype(jnp.float32), 0)
    grad_active = jnp.dot(grad_branch_two, down_back.T, preferred_element_type=jnp.float32)
    hidden_value, gelu_pull = jax.vjp(jax.nn.gelu, hidden)
    grad_hidden = gelu_pull(grad_active)[0].astype(jnp.bfloat16)
    grad_up = jnp.dot(normed_two_low.T, grad_hidden, preferred_element_type=jnp.float32)
    grad_up_bias = jnp.sum(grad_hidden.astype(jnp.float32), 0)
    grad_normed_two = jnp.dot(grad_hidden, up_back.T, preferred_element_type=jnp.float32)
    grad_mid_norm, grad_gain_two, grad_bias_two = norm_back(
        grad_normed_two, normal_two, inverse_two, gain_two_back.astype(jnp.float32)
    )
    grad_middle = grad_result + grad_mid_norm
    grad_branch = (keep_rows * grad_middle).astype(jnp.bfloat16)
    grad_out_weight = jnp.dot(mixed_rows.T, grad_branch, preferred_element_type=jnp.float32)
    grad_out_bias = jnp.sum(grad_branch.astype(jnp.float32), 0)
    grad_mixed = jnp.dot(grad_branch, out_back.T, preferred_element_type=jnp.float32).astype(
        jnp.bfloat16
    )

    def head_backward(head_item):
        query_head, key_head, value_head, grad_head, lse_head = head_item
        scores = masked_scores(query_head, key_head, same_seq, score_scale)
        softmax_rows = jnp.exp(scores - lse_head)
        grad_value = jnp.dot(
            softmax_rows.astype(jnp.bfloat16).T, grad_head, preferred_element_type=jnp.float32
        )
        grad_softmax = jnp.dot(grad_head, value_head.T, preferred_element_type=jnp.float32)
        inner_sum = jnp.sum(grad_softmax * softmax_rows, -1, keepdims=True)
        grad_scores = (softmax_rows * (grad_softmax - inner_sum)).astype(jnp.bfloat16)
        grad_query = (
            jnp.dot(grad_scores, key_head, preferred_element_type=jnp.float32) * score_scale
        )
        grad_key = (
            jnp.dot(grad_scores.T, query_head, preferred_element_type=jnp.float32) * score_scale
        )
        return (grad_query, grad_key, grad_value)

    grad_query_heads, grad_key_heads, grad_value_heads = lax.map(
        head_backward, (query_heads, key_heads, value_heads, split_heads(grad_mixed), log_total)
    )
    grad_packed = jnp.concatenate(
        [join_heads(grad_query_heads), join_heads(grad_key_heads), join_heads(grad_value_heads)], 1
    ).astype(jnp.bfloat16)
    grad_qkv = jnp.dot(normed_low.T, grad_packed, preferred_element_type=jnp.float32)
    grad_query_bias = jnp.sum(grad_packed[:, :model_width].astype(jnp.float32), 0)
    grad_value_bias = jnp.sum(grad_packed[:, 2 * model_width :].astype(jnp.float32), 0)
    grad_normed = jnp.dot(grad_packed, qkv_back.T, preferred_element_type=jnp.float32)
    grad_in_norm, grad_gain_one, grad_bias_one = norm_back(
        grad_normed, normal_one, inverse_one, gain_one_back.astype(jnp.float32)
    )
    grad_tokens = (grad_middle + grad_in_norm).astype(jnp.bfloat16)
    summed = (
        lax.psum_scatter(grad_gain_one, "dp", scatter_dimension=0, tiled=True),
        lax.psum_scatter(grad_bias_one, "dp", scatter_dimension=0, tiled=True),
        lax.psum_scatter(grad_qkv, "dp", scatter_dimension=0, tiled=True),
        lax.psum_scatter(grad_query_bias, "dp", scatter_dimension=0, tiled=True),
        lax.psum_scatter(grad_value_bias, "dp", scatter_dimension=0, tiled=True),
        lax.psum_scatter(grad_out_weight, "dp", scatter_dimension=0, tiled=True),
        lax.psum_scatter(grad_out_bias, "dp", scatter_dimension=0, tiled=True),
        lax.psum_scatter(grad_gain_two, "dp", scatter_dimension=0, tiled=True),
        lax.psum_scatter(grad_bias_two, "dp", scatter_dimension=0, tiled=True),
        lax.psum_scatter(grad_up, "dp", scatter_dimension=0, tiled=True),
        lax.psum_scatter(grad_up_bias, "dp", scatter_dimension=0, tiled=True),
        lax.psum_scatter(grad_down, "dp", scatter_dimension=0, tiled=True),
        lax.psum_scatter(grad_down_bias, "dp", scatter_dimension=0, tiled=True),
    )
    return (
        result.astype(jnp.bfloat16),
        grad_tokens,
        summed[0],
        summed[1],
        summed[2],
        summed[3],
        summed[4],
        summed[5],
        summed[6],
        summed[7],
        summed[8],
        summed[9],
        summed[10],
        summed[11],
        summed[12],
    )


def solution(mesh):
    placed = (
        P("dp", None),
        P("dp"),
        P("dp"),
        P("dp"),
        P("dp", None),
        P("dp"),
        P("dp"),
        P("dp", None),
        P("dp"),
        P("dp"),
        P("dp"),
        P("dp", None),
        P("dp"),
        P("dp", None),
        P("dp"),
        P("dp", None),
    )
    return jax.shard_map(
        local,
        mesh=mesh,
        in_specs=placed,
        out_specs=(
            P("dp", None),
            P("dp", None),
            P("dp"),
            P("dp"),
            P("dp", None),
            P("dp"),
            P("dp"),
            P("dp", None),
            P("dp"),
            P("dp"),
            P("dp"),
            P("dp", None),
            P("dp"),
            P("dp", None),
            P("dp"),
        ),
        check_vma=False,
    )
```

profile of v0, /device:TPU:0, one launch (start us, length us, event | category | flops | bytes accessed | tf_op | source)
XLA Modules:
  0.0 874.0 jit_solution(18269189886685151966)
XLA Ops:
  17.6 42.8 %all-reduce.19 = (bf16[768]{0:T(1024)(128)(2,1)S(1)}, bf16[768]{0:T(1024)(128)(2,1)S(1)}, bf16[768]{0:T(1024)(128)(2,1)S(1)}, bf16[768]{0:T(1024)(128)(2,1)S(1)}...) all-reduce(bf16[768]{0:T(1024)(128)(2,1)S(1)} %dynamic-update-slice, ...), channel_id=1, replica_groups=mesh['dp'=32] {'dp'}, use_global_device_ids=true, to_apply=%add.1 | all-reduce | flops 9216 | bytes 36864
  64.8 9.1 %all-gather.5.cloned.1.call-done = bf16[768,2304]{1,0:T(8,128)(2,1)} async-done(((bf16[24,2304]{1,0:T(8,128)(2,1)}), bf16[768,2304]{1,0:T(8,128)(2,1)}) %all-gather.5.cloned.1.call-update) | async-done | bytes 3538960 | tf_op jit(solution)/shard_map/all_gather | solution.py:70
  73.9 6.3 fusion.85
  90.6 4.1 copy.69
  97.3 4.1 copy.68
  102.8 68.8 %while.28 = (s32[]{:T(128)}, bf16[12,1024,64]{1,2,0:T(8,128)(2,1)}, f32[12,1024,1]{1,2,0:T(1,128)S(1)}, bf16[12,1024,64]{2,1,0:T(8,128)(2,1)S(1)}, bf16[12,1024,...) while((s32[]{:T(128)}, bf16[12,1024,64]{1,2,0:T(8,128)(2,1)}, ...), condition=%wide.region_5.6_spmd.clone, body=%wide.region_2.5_spmd.clone.sunk | while | flops 284163072 | bytes 13695065 | solution.py:134
  177.5 17.8 %all-gather.9.cloned.1.call-done = bf16[768,3072]{1,0:T(8,128)(2,1)} async-done(((bf16[24,3072]{1,0:T(8,128)(2,1)}), bf16[768,3072]{1,0:T(8,128)(2,1)}) %all-gather.9.cloned.1.call-update) | async-done | bytes 4718608 | tf_op jit(solution)/shard_map/all_gather | solution.py:77
  195.3 10.6 %fusion.88 = f32[1024,3072]{1,0:T(8,128)} fusion(bf16[768,3072]{1,0:T(8,128)(2,1)} %all-gather.9.cloned.1.call-done, f32[1024,768]{0,1:T(8,128)S(1)} %get-tuple-element.299, f32[768]{0:T(1024)S(1)} %convert_element_type.120, f32[768]{0:T(1024)S(1)} %convert_element_type.119, f32[1024]{0:T(1024)S(1)} %add_rsqrt_fusion, f32[1024]{0:T(1024)S(1)} %broadcast_multiply_fusion.4), kind=kOutput, calls=%fused_computation.125 | convolution fusion | flops 4835770368 | bytes 20461568 | tf_op jit(solution)/shard_map/dot_general | solution.py:144
  205.9 54.6 %all-gather.11.cloned.1.call-done = bf16[3072,768]{1,0:T(8,128)(2,1)} async-done(((bf16[96,768]{1,0:T(8,128)(2,1)}), bf16[3072,768]{1,0:T(8,128)(2,1)}) %all-gather.11.cloned.1.call-update) | async-done | bytes 4718608 | tf_op jit(solution)/shard_map/all_gather | solution.py:79
  260.6 17.1 %convert_reduce_fusion = (f32[3072]{0:T(1024)S(1)}, bf16[1024,3072]{1,0:T(8,128)(2,1)S(1)}) fusion(f32[1024,3072]{1,0:T(8,128)} %fusion.88, f32[3072]{0:T(1024)S(1)} %convert_element_type.122, bf16[3072,768]{1,0:T(8,128)(2,1)} %all-gather.11.cloned.1.call-done, bf16[1024,768]{0,1:T(8,128)(2,1)} %copy.71, f32[1024]{0:T(1024)S(1)} %compare_convert_fusion), kind=kOutput, calls=%fused_computation.66 | convolution fusion | flops 4906546176 | bytes 25194496 | tf_op jit(solution)/shard_map/dot_general | solution.py:173
  277.7 6.8 fusion.91
  294.6 4.3 fusion.92
  299.0 4.3 convolution_convert_fusion
  303.3 4.2 copy.73
  311.5 142.4 %while.29 = (s32[]{:T(128)}, bf16[12,1024,64]{1,2,0:T(8,128)(2,1)}, bf16[12,1024,64]{1,2,0:T(8,128)(2,1)}, bf16[12,1024,64]{1,2,0:T(8,128)(2,1)}, bf16[12,1024,6...) while((s32[]{:T(128)}, bf16[12,1024,64]{1,2,0:T(8,128)(2,1)}, ...), condition=%wide.region_12.13_spmd.clone, body=%wide.region_10.12_spmd.clone.sunk | while | flops 681704448 | bytes 34112624 | solution.py:208
  454.0 9.9 %fusion.77 = f32[768,2304]{1,0:T(8,128)} fusion(bf16[1024,768]{0,1:T(8,128)(2,1)} %bitcast.18, bf16[1024,768]{0,1:T(8,128)(2,1)} %bitcast.136, bf16[1024,768]{0,1:T(8,128)(2,1)} %bitcast.131, bf16[1024,768]{0,1:T(8,128)(2,1)} %copy-done.1, f32[768]{0:T(1024)S(1)} %copy-done.16, f32[768]{0:T(1024)S(1)} %copy-done.12, f32[1024]{0:T(1024)S(1)} %copy-done.14, ...), kind=kOutput, calls=%fused_computation.108 | convolution fusion | flops 3642753024 | bytes 13383680 | tf_op jit(solution)/shard_map/dot_general | solution.py:214
  463.9 10.5 %fusion.87 = f32[768,3072]{1,0:T(8,128)} fusion(bf16[1024,3072]{1,0:T(8,128)(2,1)} %copy-done.18, f32[1024,768]{0,1:T(8,128)S(1)} %get-tuple-element.299, f32[768]{0:T(1024)S(1)} %convert_element_type.120, f32[768]{0:T(1024)S(1)} %convert_element_type.119, f32[1024]{0:T(1024)S(1)} %add_rsqrt_fusion, f32[1024]{0:T(1024)S(1)} %broadcast_multiply_fusion.4), kind=kOutput, calls=%fused_computation.124 | convolution fusion | flops 4835770368 | bytes 18888704 | tf_op jit(solution)/shard_map/dot_general | solution.py:176
  474.5 14.9 %fusion.79 = f32[3072,768]{1,0:T(8,128)} fusion(bf16[1024,768]{0,1:T(8,128)(2,1)} %copy.71, f32[1024]{0:T(1024)S(1)} %compare_convert_fusion, f32[1024,3072]{1,0:T(8,128)} %fusion.88, f32[3072]{0:T(1024)S(1)} %convert_element_type.122), kind=kOutput, calls=%fused_computation.111 | convolution fusion | flops 4865654784 | bytes 23609344 | tf_op jit(solution)/shard_map/dot_general | solution.py:171
  490.1 9.2 %fusion.90 = (f32[768]{0:T(1024)S(1)}, f32[1024,768]{1,0:T(8,128)}) fusion(bf16[768,2304]{1,0:T(8,128)(2,1)} %all-gather.5.cloned.1.call-done, bf16[1024,768]{0,1:T(8,128)(2,1)} %bitcast.18, bf16[1024,768]{0,1:T(8,128)(2,1)} %bitcast.137, bf16[1024,768]{0,1:T(8,128)(2,1)} %bitcast.132), kind=kOutput, calls=%fused_computation.127 | convolution fusion | flops 3638820096 | bytes 11406336 | tf_op jit(solution)/shard_map/dot_general | solution.py:217
  509.5 42.0 %all-reduce.18 = (f32[768]{0:T(1024)S(1)}, f32[768]{0:T(1024)S(1)}, f32[768]{0:T(1024)S(1)}, f32[768]{0:T(1024)S(1)}, f32[768]{0:T(1024)S(1)}, /*index=5*/f32[76...) all-reduce(f32[768]{0:T(1024)S(1)} %get-tuple-element.233, ...), channel_id=2, replica_groups=mesh['dp'=32] {'dp'}, use_global_device_ids=true, to_apply=%region_16.17.clone | all-reduce | flops 9216 | bytes 73728
  556.2 5.8 fusion.71
  564.6 11.9 %add_convert_fusion = bf16[1024,768]{0,1:T(8,128)(2,1)} fusion(f32[1024,768]{0,1:T(8,128)S(1)} %get-tuple-element.299, bf16[3072,768]{1,0:T(8,128)(2,1)} %all-gather.11.cloned.1.call-done, f32[768]{0:T(1024)S(1)} %convert_element_type.124, f32[1024]{0:T(1024)S(1)} %compare_convert_fusion, f32[1024,3072]{1,0:T(8,128)} %fusion.88, ...), kind=kOutput, calls=%fused_computation.102 | convolution fusion | flops 4866441216 | bytes 22039552 | tf_op jit(solution)/shard_map/dot_general | solution.py:149
  583.4 141.2 %reduce-scatter.9.cloned.1.call-done = f32[24,3072]{1,0:T(8,128)} async-done(((f32[768,3072]{1,0:T(8,128)}), f32[24,3072]{1,0:T(8,128)}) %reduce-scatter.9.cloned.1.call-update) | async-done | bytes 294928 | tf_op jit(solution)/shard_map/reduce_scatter | solution.py:232
  724.6 142.2 %reduce-scatter.11.cloned.1.call-done = f32[96,768]{1,0:T(8,128)} async-done(((f32[3072,768]{1,0:T(8,128)}), f32[96,768]{1,0:T(8,128)}) %reduce-scatter.11.cloned.1.call-update) | async-done | bytes 294928 | tf_op jit(solution)/shard_map/reduce_scatter | solution.py:234
  (271 shorter events, 284.5 us)
Async XLA Ops:
  7.2 66.7 %all-gather.5.cloned.1.call-start = ((), (), s32[]{:S(2)}) async-start(), calls=%async_computation.4 | async-start | bytes 3649536 | tf_op jit(solution)/shard_map/all_gather | solution.py:70
  7.9 163.6 %all-gather.7.cloned.1.call-start = ((), (), s32[]{:S(2)}) async-start(), calls=%async_computation.5 | async-start | bytes 1216512 | tf_op jit(solution)/shard_map/all_gather | solution.py:73
  8.7 186.7 %all-gather.9.cloned.1.call-start = ((), (), s32[]{:S(2)}) async-start(), calls=%async_computation.6 | async-start | bytes 4866048 | tf_op jit(solution)/shard_map/all_gather | solution.py:77
  9.4 251.2 %all-gather.11.cloned.1.call-start = ((), (), s32[]{:S(2)}) async-start(), calls=%async_computation.7 | async-start | bytes 4866048 | tf_op jit(solution)/shard_map/all_gather | solution.py:79
  10.0 569.6 %reduce-scatter.7.cloned.1.call-start = ((), (), s32[]{:S(2)}) async-start(), calls=%async_computation.9 | async-start | bytes 2433024 | tf_op jit(solution)/shard_map/reduce_scatter | solution.py:228
  60.4 13.5 %copy-start.11 = (f32[768]{0:T(1024)}, f32[768]{0:T(1024)S(1)}, u32[]{:S(2)}) copy-start(f32[768]{0:T(1024)S(1)} %convert_element_type.108) | copy-start | bytes 9220
  60.4 13.5 %copy-start.15 = (f32[768]{0:T(1024)}, f32[768]{0:T(1024)S(1)}, u32[]{:S(2)}) copy-start(f32[768]{0:T(1024)S(1)} %convert_element_type.109) | copy-start | bytes 9220
  60.4 2.7 copy-start.8
  60.5 2.7 copy-start.7
  62.3 11.6 %copy-start.1 = (bf16[1024,768]{0,1:T(8,128)(2,1)}, bf16[1024,768]{0,1:T(8,128)(2,1)S(1)}, u32[]{:S(2)}) copy-start(bf16[1024,768]{0,1:T(8,128)(2,1)S(1)} %copy.63) | copy-start | bytes 4718596
  62.6 17.6 %copy-start.9 = (f32[1024]{0:T(1024)}, f32[1024]{0:T(1024)S(1)}, u32[]{:S(2)}) copy-start(f32[1024]{0:T(1024)S(1)} %broadcast_multiply_fusion.5) | copy-start | bytes 12292
  63.1 17.1 %copy-start.13 = (f32[1024]{0:T(1024)}, f32[1024]{0:T(1024)S(1)}, u32[]{:S(2)}) copy-start(f32[1024]{0:T(1024)S(1)} %add_rsqrt_fusion.1) | copy-start | bytes 12292
  260.6 17.1 %copy-start.5 = (bf16[768,3072]{1,0:T(8,128)(2,1)S(1)}, bf16[768,3072]{1,0:T(8,128)(2,1)}, u32[]{:S(2)}) copy-start(bf16[768,3072]{1,0:T(8,128)(2,1)} %all-gather.9.cloned.1.call-done) | copy-start | bytes 14155780
  277.7 6.8 copy-start.18
  288.2 3.1 copy-start
  288.2 3.3 copy-start.3
  299.0 284.4 %reduce-scatter.5.cloned.1.call-start = ((), (), s32[]{:S(2)}) async-start(), calls=%async_computation.8 | async-start | bytes 7299072 | tf_op jit(solution)/shard_map/reduce_scatter | solution.py:225
  311.5 142.4 %copy-start.10 = (f32[1024]{0:T(1024)S(1)}, f32[1024]{0:T(1024)}, u32[]{:S(2)}) copy-start(f32[1024]{0:T(1024)} %copy-done.9) | copy-start | bytes 12292
  311.5 142.4 %copy-start.12 = (f32[768]{0:T(1024)S(1)}, f32[768]{0:T(1024)}, u32[]{:S(2)}) copy-start(f32[768]{0:T(1024)} %copy-done.11) | copy-start | bytes 9220
  311.5 142.4 %copy-start.14 = (f32[1024]{0:T(1024)S(1)}, f32[1024]{0:T(1024)}, u32[]{:S(2)}) copy-start(f32[1024]{0:T(1024)} %copy-done.13) | copy-start | bytes 12292
  311.5 142.4 %copy-start.16 = (f32[768]{0:T(1024)S(1)}, f32[768]{0:T(1024)}, u32[]{:S(2)}) copy-start(f32[768]{0:T(1024)} %copy-done.15) | copy-start | bytes 9220
  463.9 260.7 %reduce-scatter.9.cloned.1.call-start = ((), (), s32[]{:S(2)}) async-start(), calls=%async_computation.10 | async-start | bytes 9732096 | tf_op jit(solution)/shard_map/reduce_scatter | solution.py:232
  474.5 392.3 %reduce-scatter.11.cloned.1.call-start = ((), (), s32[]{:S(2)}) async-start(), calls=%async_computation.11 | async-start | bytes 9732096 | tf_op jit(solution)/shard_map/reduce_scatter | solution.py:234
  503.0 3.5 copy-start.2
  (3 other events, 3.5 us)
Sparse Core Ops, SparseCore 0:
  10.9 62.9 all-gather.4
  76.8 52.9 all-gather.6
  132.8 62.5 all-gather.8
  198.1 62.4 all-gather.10
  299.1 97.8 reduce-scatter.6
  464.0 119.2 reduce-scatter.4
  589.8 134.6 reduce-scatter.8
  732.0 134.6 reduce-scatter.10
where the time goes:
time: 885 us; the launch traced here: 874 us
  waiting for transfers between devices  371 us (42%)
  matrix products  294 us (33%)
  blocking collectives  84.8 us (10%)
  local copies, waits for them, and re-layouts  61.6 us (7%)
  other arithmetic  46.5 us (5%)
  between operations  14.9 us (2%)
    reduce_scatter x1, waiting for transfers between devices, local(): lax.psum_scatter(grad_down, 'dp', scatter_dimension=0, tiled=True)  142 us
    reduce_scatter x1, waiting for transfers between devices, local(): lax.psum_scatter(grad_up, 'dp', scatter_dimension=0, tiled=True)  141 us
    unnamed x2, blocking collectives  84.8 us
    all_gather x1, waiting for transfers between devices, local(): lax.all_gather(shards[11], 'dp', axis=0, tiled=True)  54.6 us
    dot_general x24, matrix products, masked_scores(): jnp.dot(query_head, key_head.T, preferred_element_type=jnp.float32)  44.7 us
    unnamed x72, local copies, waits for them, and re-layouts  36.5 us
    dot_general x12, matrix products, head_forward(): jnp.dot(softmax_rows, value_head, preferred_element_type=jnp.float32)  35.5 us
    dot_general x12, matrix products, head_backward(): jnp.dot(grad_scores.T, query_head, preferred_element_type=jnp.float32)  28.6 us
  transfers between devices with their start and end apart: 8, of which 6 were waited for; matrix products, arithmetic and copies ran while one was open for 41% of the time, Pallas kernels for 0%

commit v1 on v0

v1 whole, which is shorter than its diff:
```python
import functools

import jax
import jax.numpy as jnp
from jax import lax
from jax.experimental import pallas as pl
from jax.experimental.pallas import tpu as pltpu
from jax.sharding import PartitionSpec as P

HEADS = 12
EPSILON = 1e-06
LOG2E = 1.4426950408889634
BF = jnp.bfloat16
F32 = jnp.float32
RUNS = 6
SLICES = 4
SMALL = 256
WINDOW = 384
PAIRS = 6
BLANK = -8e9
NOTHING = 5e8
VMEM_BYTES = 28 * 1024 * 1024

IN_VMEM = pl.BlockSpec(memory_space=pltpu.VMEM)
IN_SMEM = pl.BlockSpec(memory_space=pltpu.SMEM)


def shape_of(shape, dtype):
    return jax.ShapeDtypeStruct(shape, dtype)


def params(**more):
    return pltpu.CompilerParams(vmem_limit_bytes=VMEM_BYTES, **more)


def cost(flops, moved, exps=0):
    return pl.CostEstimate(flops=int(flops), bytes_accessed=int(moved), transcendentals=int(exps))


def mm(left, right):
    return lax.dot_general(left, right, (((1,), (0,)), ((), ())), preferred_element_type=F32)


def mm_nt(left, right):
    return lax.dot_general(left, right, (((1,), (1,)), ((), ())), preferred_element_type=F32)


def chosen(mask, yes, no):
    return jnp.where(mask, yes.astype(F32), no.astype(F32)).astype(BF)


def turned(matrix):
    return jnp.transpose(matrix.astype(F32)).astype(BF)


def rows_below(base, size, limit):
    return base + lax.broadcasted_iota(jnp.int32, (size, 1), 0) < limit


def normalize(values):
    center = values - jnp.mean(values, -1, keepdims=True)
    spread = jnp.mean(center * center, -1, keepdims=True)
    inverse = lax.rsqrt(spread + EPSILON)
    return center * inverse, inverse


def kept_rows(counts):
    total = counts[0]
    for label in range(1, RUNS - 1):
        total = total + counts[label]
    return total


def chip_at(index, order):
    if order == "yxz":
        return (index & 3) * 4 + (index >> 3) * 2 + ((index >> 2) & 1)
    if order == "xyz":
        return (index & 3) * 4 + ((index >> 2) & 1) * 2 + (index >> 3)
    return index


def place_at(offset, order):
    if order == "yxz":
        return ((offset >> 1) & 1) * 8 + (offset & 1) * 4 + (offset >> 2)
    if order == "xyz":
        return (offset & 1) * 8 + ((offset >> 1) & 1) * 4 + (offset >> 2)
    return offset


def lay(source, chip, order, store):
    blocks, blk = source.shape[:2]
    for index in range(blocks):
        store(slice(index * blk, (index + 1) * blk), source[place_at(index ^ chip, order)])


def hand(values, at, target, half, chip, order):
    blk = target.shape[2]
    for index in range(values.shape[0] // blk):
        place = place_at((at // blk + index) ^ chip, order)
        target[half, place, :, : values.shape[1]] = values[index * blk : (index + 1) * blk]


def qkv_kernel(
    spot, x_ref, ta0, ta1, tb0, tb1, a1t_ref, q_ref, k_ref, v_ref, wq, wk, wv, wo, small_ref, first_s, second_s, *, orders
):
    core, chip = spot[0], spot[1]
    rows, width = x_ref.shape

    table = second_s
    lay(ta0, chip, orders[0], lambda here, value: _put(first_s, table, core, here, value, width))
    lay(ta1, chip, orders[0], lambda here, value: _put(first_s, table, 1 - core, here, value, width))
    wq[...] = first_s[0]
    wv[...] = first_s[1]
    small = jnp.transpose(table[0].astype(F32))
    small_ref[...] = small[: small_ref.shape[0], :]
    lay(tb0, chip, orders[1], lambda here, value: _put(first_s, None, core, here, value, width))
    lay(tb1, chip, orders[1], lambda here, value: _put(first_s, None, 1 - core, here, value, width))
    wk[...] = first_s[0]
    wo[...] = first_s[1]
    gain, bias = small_ref[0:1, :], small_ref[1:2, :]
    bias_query, bias_value = small_ref[2:3, :], small_ref[3:4, :]
    step = 256
    for at in range(0, rows, step):
        here = slice(at, at + step)
        normal, _ = normalize(x_ref[here, :].astype(F32))
        a1 = (normal * gain + bias).astype(BF)
        a1t_ref[:, here] = jnp.transpose(normal * gain + bias).astype(BF)
        q_ref[here, :] = (mm(a1, wq[...]) + bias_query).astype(BF)
        k_ref[here, :] = mm(a1, wk[...]).astype(BF)
        v_ref[here, :] = (mm(a1, wv[...]) + bias_value).astype(BF)


def _put(main, table, half, here, value, width):
    main[half, here, :] = value[:, :width]
    if table is not None:
        table[half, here, :] = value[:, width:]


def qkv_call(spot, x, ta, tb, orders):
    rows, width = x.shape
    act, weight = shape_of((rows, width), BF), shape_of((width, width), BF)
    return pl.pallas_call(
        functools.partial(qkv_kernel, orders=orders),
        out_shape=(shape_of((width, rows), BF),) + (act,) * 3 + (weight,) * 4 + (shape_of((16, width), F32),),
        in_specs=[IN_SMEM] + [IN_VMEM] * 5,
        out_specs=(IN_VMEM,) * 9,
        scratch_shapes=[pltpu.VMEM((2, width, width), BF), pltpu.VMEM((2, width, SMALL), BF)],
        compiler_params=params(),
        cost_estimate=cost(6 * rows * width * width, 16 * width * width),
        name="norm_qkv",
    )(spot, x, *ta, *tb)


def lane_of(size):
    return lax.broadcasted_iota(jnp.int32, (size, 128), 1)


def for_runs(counts, rows, visit):
    def body(run, start):
        size = counts[run]
        end = start + size
        base = (start // 16) * 16
        span = end - base

        def windowed(window):
            at = jnp.minimum(base, rows - window)
            visit(at, window, at, window, start, end, start, end, run)

        pl.when((size > 0) & (span <= 128))(lambda: windowed(128))
        pl.when((span > 128) & (span <= 256))(lambda: windowed(256))
        pl.when((span > 256) & (span <= WINDOW))(lambda: windowed(WINDOW))

        @pl.when(span > WINDOW)
        def _():
            def part(index, carry):
                low = base + index * 128
                at = jnp.minimum(low, rows - 128)
                visit(at, 128, 0, rows, jnp.maximum(low, start), end, start, end, RUNS + index)
                return carry

            lax.fori_loop(0, (span + 127) // 128, part, 0)

        return end

    lax.fori_loop(0, RUNS, body, 0)


def inside(base, size, low, high, axis=0):
    shape = (size, 128) if axis == 0 else (1, size)
    place = base + lax.broadcasted_iota(jnp.int32, shape, axis)
    return (place >= low) & (place < high)


def marked(q_two, k_two, k_ok, head):
    spare = 64 if head == 0 else 0
    q_lane, k_lane = lane_of(q_two.shape[0]), lane_of(k_two.shape[0])
    q_half = (q_lane < 64) if head == 0 else (q_lane >= 64)
    one = jnp.where(q_lane == spare, 1.0, 0.0)
    bias = jnp.where(k_ok, 0.0, BLANK)
    return chosen(q_half, q_two, one), chosen(k_lane == spare, bias, k_two)


def attend_kernel(counts, q_ref, k_ref, v_ref, o_ref, lse_ref, *, scale):
    rows, width = q_ref.shape
    factor = scale * LOG2E

    def visit(q_base, q_size, k_base, k_size, q_low, q_high, k_low, k_high, slot):
        q_at, k_at = pl.ds(pl.multiple_of(q_base, 16), q_size), pl.ds(pl.multiple_of(k_base, 16), k_size)
        q_ok, k_ok = inside(q_base, q_size, q_low, q_high), inside(k_base, k_size, k_low, k_high)
        q_row_ok = inside(q_base, q_size, q_low, q_high, 1)

        def group(index, carry):
            heads = []
            for pair in range(PAIRS):
                lanes = pl.ds(pl.multiple_of((index * PAIRS + pair) * 128, 128), 128)
                q_two, k_two = q_ref[q_at, lanes], k_ref[k_at, lanes]
                for head in range(2):
                    q_own, k_own = marked(q_two, k_two, k_ok, head)
                    heads.append(mm_nt(k_own, q_own))
            weights, totals = [], []
            for at, scores in enumerate(heads):
                top = jnp.max(scores, 0, keepdims=True)
                weight = jnp.exp2((scores - top) * factor)
                total = jnp.sum(weight, 0, keepdims=True)
                lse = jnp.where(q_row_ok, top * factor + jnp.log2(total), NOTHING)
                lse_ref[slot, index, at : at + 1, :q_size] = lse
                weights.append(weight.astype(BF))
                totals.append(1.0 / total)
            for pair in range(PAIRS):
                lanes = pl.ds(pl.multiple_of((index * PAIRS + pair) * 128, 128), 128)
                v_turned = turned(v_ref[k_at, lanes])
                mixed = []
                for head in range(2):
                    at = 2 * pair + head
                    mixed.append(mm(v_turned[head * 64 : head * 64 + 64], weights[at]) * totals[at])
                mixed = jnp.transpose(jnp.concatenate(mixed, 0))
                o_ref[q_at, lanes] = chosen(q_ok, mixed, o_ref[q_at, lanes])
            return carry

        lax.fori_loop(0, width // 128 // PAIRS, group, 0)

    for_runs(counts, rows, visit)


def attend_call(counts, q, k, v):
    rows, width = q.shape
    return pl.pallas_call(
        functools.partial(attend_kernel, scale=(width // HEADS) ** -0.5),
        out_shape=(shape_of((rows, width), BF), shape_of((RUNS + rows // 128, width // 128 // PAIRS, 16, WINDOW), F32)),
        in_specs=[IN_SMEM] + [IN_VMEM] * 3,
        out_specs=(IN_VMEM, IN_VMEM),
        compiler_params=params(),
        cost_estimate=cost(8 * rows * 256 * width, 8 * rows * width, HEADS * rows * 256),
        name="attend",
    )(counts, q, k, v)


def attend_back_kernel(
    counts, q_ref, k_ref, v_ref, g_ref, lse_ref, dq_ref, dk_ref, dv_ref, dk_sum, dv_sum, *, scale
):
    rows, width = q_ref.shape
    factor = scale * LOG2E

    def visit(q_base, q_size, k_base, k_size, q_low, q_high, k_low, k_high, slot):
        q_at, k_at = pl.ds(pl.multiple_of(q_base, 16), q_size), pl.ds(pl.multiple_of(k_base, 16), k_size)
        q_ok, k_ok = inside(q_base, q_size, q_low, q_high), inside(k_base, k_size, k_low, k_high)
        whole = q_size == k_size
        def group(index, carry):
            spans = [pl.ds(pl.multiple_of((index * PAIRS + pair) * 128, 128), 128) for pair in range(PAIRS)]
            g_lane, k_first = lane_of(q_size), lane_of(k_size) < 64
            scores, slopes = [], []
            for lanes in spans:
                q_two, k_two, v_two, g_two = q_ref[q_at, lanes], k_ref[k_at, lanes], v_ref[k_at, lanes], g_ref[q_at, lanes]
                for head in range(2):
                    q_own, k_own = marked(q_two, k_two, k_ok, head)
                    g_half = (g_lane < 64) if head == 0 else (g_lane >= 64)
                    scores.append(mm_nt(k_own, q_own))
                    slopes.append(mm_nt(v_two, jnp.where(g_half, g_two.astype(F32), 0.0).astype(BF)))
            probs = []
            for at in range(2 * PAIRS):
                lse = lse_ref[slot, index, at : at + 1, :q_size]
                prob = jnp.exp2(scores[at] * factor - lse)
                slope = prob * slopes[at]
                slopes[at] = (slope - prob * jnp.sum(slope, 0, keepdims=True)).astype(BF)
                probs.append(prob.astype(BF))
            for pair, lanes in enumerate(spans):
                two = (2 * pair, 2 * pair + 1)
                k_turned = turned(k_ref[k_at, lanes])
                dvs = [mm(probs[at], g_ref[q_at, lanes]) for at in two]
                dks = [mm(slopes[at], q_ref[q_at, lanes]) for at in two]
                dqs = [mm(k_turned[at % 2 * 64 : at % 2 * 64 + 64], slopes[at]) for at in two]
                dq = jnp.transpose(jnp.concatenate(dqs, 0)) * scale
                dq_ref[q_at, lanes] = chosen(q_ok, dq, dq_ref[q_at, lanes])
                dk, dv = jnp.where(k_first, dks[0], dks[1]) * scale, jnp.where(k_first, dvs[0], dvs[1])
                if whole:
                    dk_ref[k_at, lanes] = chosen(k_ok, dk, dk_ref[k_at, lanes])
                    dv_ref[k_at, lanes] = chosen(k_ok, dv, dv_ref[k_at, lanes])
                else:
                    begun = slot > RUNS
                    dk = dk + jnp.where(begun, dk_sum[:, lanes], 0.0)
                    dv = dv + jnp.where(begun, dv_sum[:, lanes], 0.0)
                    dk_sum[:, lanes] = dk
                    dv_sum[:, lanes] = dv
                    dk_ref[:, lanes] = chosen(k_ok, dk, dk_ref[:, lanes])
                    dv_ref[:, lanes] = chosen(k_ok, dv, dv_ref[:, lanes])
            return carry

        lax.fori_loop(0, width // 128 // PAIRS, group, 0)

    for_runs(counts, rows, visit)


def attend_back_call(counts, q, k, v, grad, lse):
    rows, width = q.shape
    act = shape_of((rows, width), BF)
    return pl.pallas_call(
        functools.partial(attend_back_kernel, scale=(width // HEADS) ** -0.5),
        out_shape=(act, act, act),
        in_specs=[IN_SMEM] + [IN_VMEM] * 5,
        out_specs=(IN_VMEM,) * 3,
        scratch_shapes=[pltpu.VMEM((rows, width), F32), pltpu.VMEM((rows, width), F32)],
        compiler_params=params(),
        cost_estimate=cost(20 * rows * 256 * width, 18 * rows * width, HEADS * rows * 256),
        name="attend_back",
    )(counts, q, k, v, grad, lse)


def out_kernel(counts, o_ref, x_ref, w_ref, small_ref, cot_ref, y_ref, a2_ref, a2t_ref, ot_ref, gm_ref):
    limit = kept_rows(counts)
    out_bias, gain, bias = small_ref[4:5, :], small_ref[5:6, :], small_ref[6:7, :]
    step = 256
    for at in range(0, o_ref.shape[0], step):
        here = slice(at, at + step)
        valid = rows_below(at, step, limit)
        gm_ref[here, :] = jnp.where(valid, cot_ref[here, :].astype(F32), 0.0).astype(BF)
        branch = mm(o_ref[here, :], w_ref[...]) + out_bias
        middle = x_ref[here, :].astype(F32) + jnp.where(valid, branch, 0.0)
        y_ref[here, :] = middle
        a2 = normalize(middle)[0] * gain + bias
        a2_ref[here, :] = a2.astype(BF)
        a2t_ref[:, here] = jnp.transpose(a2).astype(BF)
        ot_ref[:, here] = turned(o_ref[here, :])


def out_call(counts, mixed, x, weights, small, cot):
    rows, width = x.shape
    return pl.pallas_call(
        out_kernel,
        out_shape=(
            shape_of((rows, width), F32),
            shape_of((rows, width), BF),
            shape_of((width, rows), BF),
            shape_of((width, rows), BF),
            shape_of((rows, width), BF),
        ),
        in_specs=[IN_SMEM] + [IN_VMEM] * 5,
        out_specs=(IN_VMEM,) * 5,
        compiler_params=params(),
        cost_estimate=cost(2 * rows * width * width, 10 * rows * width),
        name="out_norm",
    )(counts, mixed, x, weights, small, cot)


def feed_kernel(
    counts, spot, a2_ref, a2t_ref, gm_ref, small_ref, out_in, w0, w1, *rest, index, first, last, orders
):
    if first:
        out_ref, down_ref, grads, sums_ref = rest[:4]
        held, act_t, du_s = rest[4:]
    else:
        down_in, out_ref, down_ref, grads, sums_ref = rest[:5]
        held, act_t, du_s = rest[5:]
    core, chip = spot[0], spot[1]
    other = 1 - core
    lay(w0, chip, orders[0], lambda here, value: _put(held, None, core, here, value, value.shape[1]))
    lay(w1, chip, orders[0], lambda here, value: _put(held, None, other, here, value, value.shape[1]))
    limit = kept_rows(counts)
    up_bias = small_ref[8 + index : 9 + index, :]
    rows, width = a2_ref.shape
    step = 256
    sums = jnp.zeros((1, width), F32)
    for at in range(0, rows, step):
        here = slice(at, at + step)
        valid = rows_below(at, step, limit)
        hidden = mm(a2_ref[here, :], held[0]) + up_bias
        square = hidden * hidden
        inner = 0.7978845608028654 * hidden * (1.0 + 0.044715 * square)
        bend = jnp.tanh(inner)
        half = 0.5 * (1.0 + bend)
        act = hidden * half
        act_t[:, here] = jnp.transpose(act).astype(BF)
        act = act.astype(BF)
        slope = half + 0.5 * hidden * (1.0 - bend * bend) * (0.7978845608028654 * (1.0 + 0.134145 * square))
        du = mm_nt(gm_ref[here, :], held[1]) * slope
        du_low = du.astype(BF)
        du_s[here, :] = du_low
        sums = sums + jnp.sum(du_low.astype(F32), 0, keepdims=True)
        result = out_in[here, :] + jnp.where(valid, mm(act, held[1]), 0.0)
        if last:
            result = result + jnp.where(valid, small_ref[7:8, :], 0.0)
        out_ref[here, :] = result.astype(out_ref.dtype)
        back = mm_nt(du_low, held[0])
        if not first:
            back = back + down_in[here, :]
        down_ref[here, :] = back
    sums_ref[...] = sums
    part = width // 2
    for at in range(0, width, part):
        hand(mm(a2t_ref[at : at + part, :], du_s[...]).astype(BF), at, grads, core, chip, orders[1])
        hand(mm(act_t[at : at + part, :], gm_ref[...]).astype(BF), at, grads, other, chip, orders[1])


def feed_call(counts, spot, a2, a2t, gm, small, out_in, down_in, weights, index, orders):
    rows, width = a2.shape
    blocks, blk = weights[0].shape[:2]
    first, last = down_in is None, index == SLICES - 1
    operands = [counts, spot, a2, a2t, gm, small, out_in, *weights] + ([] if first else [down_in])
    return pl.pallas_call(
        functools.partial(feed_kernel, index=index, first=first, last=last, orders=orders),
        out_shape=(
            shape_of((rows, width), BF if last else F32),
            shape_of((rows, width), F32),
            shape_of((2, blocks, blk, width), BF),
            shape_of((1, width), F32),
        ),
        in_specs=[IN_SMEM, IN_SMEM] + [IN_VMEM] * (7 if first else 8),
        out_specs=(IN_VMEM,) * 4,
        scratch_shapes=[
            pltpu.VMEM((2, width, width), BF),
            pltpu.VMEM((width, rows), BF),
            pltpu.VMEM((rows, width), BF),
        ],
        compiler_params=params(),
        cost_estimate=cost(12 * rows * width * width, 20 * rows * width, rows * width),
        name=f"feed_slice_{'abcdefgh'[index]}",
    )(*operands)


def mid_kernel(counts, spot, y_ref, down_ref, cot_ref, ot_ref, w_ref, small_ref, dy_ref, do_ref, grad, sums_ref, db_s, *, order):
    limit = kept_rows(counts)
    gain = small_ref[5:6, :]
    rows, width = y_ref.shape
    step = 256
    sums = [jnp.zeros((1, width), F32) for _ in range(4)]
    for at in range(0, rows, step):
        here = slice(at, at + step)
        valid = rows_below(at, step, limit)
        normal, inverse = normalize(y_ref[here, :])
        back = down_ref[here, :]
        scaled = back * gain
        one = jnp.mean(scaled, -1, keepdims=True)
        two = jnp.mean(scaled * normal, -1, keepdims=True)
        cot = cot_ref[here, :].astype(F32)
        dy = cot + inverse * (scaled - one - normal * two)
        dy_ref[here, :] = dy
        db = jnp.where(valid, dy, 0.0).astype(BF)
        db_s[here, :] = db
        do_ref[here, :] = mm_nt(db, w_ref[...]).astype(BF)
        sums[0] = sums[0] + jnp.sum(db.astype(F32), 0, keepdims=True)
        sums[1] = sums[1] + jnp.sum(back * normal, 0, keepdims=True)
        sums[2] = sums[2] + jnp.sum(back, 0, keepdims=True)
        sums[3] = sums[3] + jnp.sum(jnp.where(valid, cot, 0.0), 0, keepdims=True)
    for index, row in enumerate(sums):
        sums_ref[index : index + 1, :] = row
    part = width // 2
    for at in range(0, width, part):
        hand(mm(ot_ref[at : at + part, :], db_s[...]).astype(BF), at, grad, 0, spot[1], order)
    grad[0, :, :, width:] = jnp.zeros_like(grad[0, :, :, width:])


def mid_call(counts, spot, y, down, cot, mixed, weights, small, blocks, order):
    rows, width = y.shape
    return pl.pallas_call(
        functools.partial(mid_kernel, order=order),
        out_shape=(
            shape_of((rows, width), F32),
            shape_of((rows, width), BF),
            shape_of((1, blocks, width // blocks, width + SMALL), BF),
            shape_of((4, width), F32),
        ),
        in_specs=[IN_SMEM, IN_SMEM] + [IN_VMEM] * 6,
        out_specs=(IN_VMEM,) * 4,
        scratch_shapes=[pltpu.VMEM((rows, width), BF)],
        compiler_params=params(),
        cost_estimate=cost(4 * rows * width * width, 18 * rows * width),
        name="mid_back",
    )(counts, spot, y, down, cot, mixed, weights, small)


def end_kernel(
    spot, x_ref, dy_ref, a1t_ref, dq_ref, dk_ref, dv_ref, wq, wk, wv, small_ref, mid_ref, up_ref, out_grad,
    tokens_ref, ga, gb, table_s, *, orders
):
    core, chip = spot[0], spot[1]
    other = 1 - core
    rows, width = x_ref.shape
    gb[other] = out_grad[0]
    part = width // 2
    for at in range(0, width, part):
        a1t = a1t_ref[at : at + part, :]
        hand(mm(a1t, dq_ref[...]).astype(BF), at, ga, core, chip, orders[0])
        hand(mm(a1t, dv_ref[...]).astype(BF), at, ga, other, chip, orders[0])
        hand(mm(a1t, dk_ref[...]).astype(BF), at, gb, core, chip, orders[1])
    gain = small_ref[0:1, :]
    sums = [jnp.zeros((1, width), F32) for _ in range(4)]
    step = 256
    for at in range(0, rows, step):
        here = slice(at, at + step)
        dq, dk, dv = dq_ref[here, :], dk_ref[here, :], dv_ref[here, :]
        back = mm_nt(dq, wq[...]) + mm_nt(dk, wk[...]) + mm_nt(dv, wv[...])
        normal, inverse = normalize(x_ref[here, :].astype(F32))
        scaled = back * gain
        one = jnp.mean(scaled, -1, keepdims=True)
        two = jnp.mean(scaled * normal, -1, keepdims=True)
        tokens_ref[here, :] = (dy_ref[here, :] + inverse * (scaled - one - normal * two)).astype(BF)
        sums[0] = sums[0] + jnp.sum(back * normal, 0, keepdims=True)
        sums[1] = sums[1] + jnp.sum(back, 0, keepdims=True)
        sums[2] = sums[2] + jnp.sum(dq.astype(F32), 0, keepdims=True)
        sums[3] = sums[3] + jnp.sum(dv.astype(F32), 0, keepdims=True)
    table_s[...] = jnp.zeros_like(table_s)
    for index in range(4):
        table_s[index : index + 1, :] = sums[index]
        table_s[4 + index : 5 + index, :] = mid_ref[index : index + 1, :]
        table_s[8 + index : 9 + index, :] = up_ref[index : index + 1, :]
    table = jnp.transpose(table_s[...]).astype(BF)
    blk = gb.shape[2]
    for index in range(width // blk):
        gb[core, place_at(index ^ chip, orders[1]), :, width:] = table[index * blk : (index + 1) * blk]


def end_call(spot, x, dy, a1, dq, dk, dv, wq, wk, wv, small, mid, ups, out_grad, orders):
    rows, width = x.shape
    blocks, blk = out_grad.shape[1:3]
    return pl.pallas_call(
        functools.partial(end_kernel, orders=orders),
        out_shape=(
            shape_of((rows, width), BF),
            shape_of((2, blocks, blk, width), BF),
            shape_of((2, blocks, blk, width + SMALL), BF),
        ),
        in_specs=[IN_SMEM] + [IN_VMEM] * 13,
        out_specs=(IN_VMEM,) * 3,
        scratch_shapes=[pltpu.VMEM((SMALL, width), F32)],
        compiler_params=params(),
        cost_estimate=cost(12 * rows * width * width, 18 * rows * width),
        name="qkv_norm_back",
    )(spot, x, dy, a1, dq, dk, dv, wq, wk, wv, small, mid, ups, out_grad)


def assemble(own, oth, spot, order):
    core, chip = spot[0], spot[1]
    blocks, blk, W = own.shape
    idx = jnp.array([place_at(a, order) for a in range(blocks)])
    pos = idx[jnp.arange(blocks) ^ chip]
    o, t = own[pos].reshape(-1, W), oth[pos].reshape(-1, W)
    return jnp.where(core == 0, o, t), jnp.where(core == 0, t, o)


def scatter_form(zero, one, spot, order, blocks):
    core, chip = spot[0], spot[1]
    W = zero.shape[1]
    src = jnp.array([chip_at(p, order) for p in range(blocks)]) ^ chip
    z, o = zero.reshape(blocks, -1, W)[src], one.reshape(blocks, -1, W)[src]
    return jnp.where(core == 0, jnp.stack([z, o]), jnp.stack([o, z]))


def x_qkv_call(spot, x, ta, tb, orders):
    width = x.shape[1]
    a0, a1w = assemble(ta[0], ta[1], spot, orders[0])
    wk, wo = assemble(tb[0], tb[1], spot, orders[1])
    wq, wv = a0[:, :width], a1w[:, :width]
    small = a0[:, width:].astype(F32).T[:16]
    n, _ = normalize(x.astype(F32))
    a1 = (n * small[0:1] + small[1:2]).astype(BF)
    return (a1.T, (mm(a1, wq) + small[2:3]).astype(BF), mm(a1, wk).astype(BF), (mm(a1, wv) + small[3:4]).astype(BF), wq, wk, wv, wo, small)


def x_out_call(counts, mixed, x, weights, small, cot):
    valid = rows_below(0, x.shape[0], kept_rows(counts))
    gm = jnp.where(valid, cot, 0).astype(BF)
    y = x.astype(F32) + jnp.where(valid, mm(mixed, weights) + small[4:5], 0.0)
    a2 = (normalize(y)[0] * small[5:6] + small[6:7]).astype(BF)
    return y, a2, a2.T, mixed.T, gm


def x_feed_call(counts, spot, a2, a2t, gm, small, out_in, down_in, weights, index, orders):
    wu, wd = assemble(weights[0], weights[1], spot, orders[0])
    valid = rows_below(0, a2.shape[0], kept_rows(counts))
    h = mm(a2, wu) + small[8 + index : 9 + index]
    act, pull = jax.vjp(jax.nn.gelu, h)
    act = act.astype(BF)
    du = pull(mm_nt(gm, wd))[0].astype(BF)
    out = out_in + jnp.where(valid, mm(act, wd), 0.0)
    last = index == SLICES - 1
    if last:
        out = (out + jnp.where(valid, small[7:8], 0.0)).astype(BF)
    back = mm_nt(du, wu) + (0 if down_in is None else down_in)
    g = scatter_form(mm(a2t, du).astype(BF), mm(act.T, gm).astype(BF), spot, orders[1], weights[0].shape[0])
    return out, back, g, jnp.sum(du.astype(F32), 0, keepdims=True)


def x_mid_call(counts, spot, y, down, cot, mixed, weights, small, blocks, order):
    valid = rows_below(0, y.shape[0], kept_rows(counts))
    n, inv = normalize(y)
    c = down * small[5:6]
    dy = cot.astype(F32) + inv * (c - jnp.mean(c, -1, keepdims=True) - n * jnp.mean(c * n, -1, keepdims=True))
    db = jnp.where(valid, dy, 0.0).astype(BF)
    do = mm_nt(db, weights).astype(BF)
    s = jnp.stack([jnp.sum(db.astype(F32), 0), jnp.sum(down * n, 0), jnp.sum(down, 0), jnp.sum(jnp.where(valid, cot.astype(F32), 0.0), 0)])
    g = jnp.pad(mm(mixed, db).astype(BF), ((0, 0), (0, SMALL)))
    core, chip = spot[0], spot[1]
    src = jnp.array([chip_at(p, order) for p in range(blocks)]) ^ chip
    return dy, do, g.reshape(blocks, -1, g.shape[1])[src][None], s


def x_end_call(spot, x, dy, a1, dq, dk, dv, wq, wk, wv, small, mid, ups, out_grad, orders):
    blocks = out_grad.shape[1]
    back = mm_nt(dq, wq) + mm_nt(dk, wk) + mm_nt(dv, wv)
    n, inv = normalize(x.astype(F32))
    c = back * small[0:1]
    tok = (dy + inv * (c - jnp.mean(c, -1, keepdims=True) - n * jnp.mean(c * n, -1, keepdims=True))).astype(BF)
    ga = scatter_form(mm(a1, dq).astype(BF), mm(a1, dv).astype(BF), spot, orders[0], blocks)
    sums = jnp.stack([jnp.sum(back * n, 0), jnp.sum(back, 0), jnp.sum(dq.astype(F32), 0), jnp.sum(dv.astype(F32), 0)])
    table = jnp.concatenate([sums, mid, ups, jnp.zeros((SMALL - 12, x.shape[1]), F32)], 0).T.astype(BF)
    gk = jnp.concatenate([mm(a1, dk).astype(BF), table], 1)
    gkb = scatter_form(gk, gk, spot, orders[1], blocks)[0]
    return tok, ga, jnp.where(spot[0] == 0, jnp.stack([gkb, out_grad[0]]), jnp.stack([out_grad[0], gkb]))


def columns(vectors):
    table = jnp.stack(vectors, 1)
    return jnp.pad(table, ((0, 0), (0, SMALL - table.shape[1])))


def flip(value, bit):
    return lax.ppermute(value, "dp", [(at, at ^ bit) for at in range(lax.axis_size("dp"))])


def pick(core, zero, one):
    return jnp.where(core == 0, zero, one)


class Staged:
    def __init__(self):
        place = lax.axis_index("dp")
        self.core = place % 2
        self.spot = jnp.stack([place % 2, place // 2]).astype(jnp.int32)
        self.blocks = lax.axis_size("dp") // 2

    def gather_order(self, index):
        return ("yxz", "xyz")[index % 2]

    def scatter_order(self, index):
        return ("xyz", "yxz")[index % 2]

    def gather(self, vectors, b_up, w_qkv, w_out, w_up, w_down):
        core = self.core
        own_rows, width = w_out.shape
        devices = width // own_rows
        ups = w_up.reshape(own_rows, devices, SLICES, own_rows).transpose(2, 0, 1, 3).reshape(SLICES, own_rows, width)
        downs = w_down.reshape(SLICES, own_rows, width)
        extra = columns(vectors + [b_up.reshape(SLICES, own_rows)[at] for at in range(SLICES)])
        zero = jnp.concatenate([w_qkv[:, :width], extra, w_qkv[:, width : 2 * width], *ups], 1)
        one = jnp.concatenate([w_qkv[:, 2 * width :], extra, w_out, *downs], 1)
        sent = pick(core, one, zero)
        kept = pick(core, zero, one)
        came = flip(sent, 1)
        both = jnp.concatenate([pick(core, kept, came), pick(core, came, kept)], 0)
        edges = [0, width + SMALL] + [width * at + SMALL for at in range(2, SLICES + 3)]
        results = []
        for index in range(SLICES + 2):
            piece = both[:, edges[index] : edges[index + 1]]
            held = jnp.stack([piece, flip(piece, 8), flip(piece, 16), flip(piece, 24)])
            for bit in ((2, 4), (4, 2))[index % 2]:
                held = jnp.concatenate([held, flip(held, bit)], 0)
            results.append((held, flip(held, 1)))
        return results

    def reduce(self, index, parts):
        def add(left, right):
            return (left.astype(F32) + right.astype(F32)).astype(BF)

        came = flip(parts[1], 1)
        held = parts[0]
        for bit in ((2, 4), (4, 2))[index % 2]:
            half = held.shape[0] // 2
            sent, held = add(held[half:], came[half:]), add(held[:half], came[:half])
            came = flip(sent, bit)
        pieces = [add(held[at], came[at]) for at in range(1, 4)]
        total = held[0].astype(F32) + came[0].astype(F32)
        for at in range(1, 4):
            total = total + flip(pieces[at - 1], 8 * at).astype(F32)
        half = total.shape[0] // 2
        kept = pick(self.core, total[:half], total[half:])
        came = flip(pick(self.core, total[half:], total[:half]), 1)
        return pick(self.core, kept, came), pick(self.core, came, kept)

    def finish(self, reduced):
        (q, v), (k_small, out) = reduced[0], reduced[1]
        width = q.shape[1]
        own_rows = q.shape[0]
        k, small = k_small[:, :width], k_small[:, width:]
        ups = jnp.stack([pair[0] for pair in reduced[2:]])
        devices = width // own_rows
        up = ups.reshape(SLICES, own_rows, devices, own_rows).transpose(1, 2, 0, 3).reshape(own_rows, SLICES * width)
        down = jnp.concatenate([pair[1] for pair in reduced[2:]], 0)
        vectors = [small[:, at] for at in range(8)]
        b_up = small[:, 8 : 8 + SLICES].T.reshape(-1)
        return vectors, b_up, jnp.concatenate([q, k, v], 1), out[:, :width], up, down


class Plain:
    def __init__(self):
        self.spot = jnp.zeros((2,), jnp.int32)
        self.blocks = 16

    def gather_order(self, index):
        return None

    def scatter_order(self, index):
        return None

    def gather(self, vectors, b_up, w_qkv, w_out, w_up, w_down):
        def whole(value):
            return lax.all_gather(value, "dp", axis=0, tiled=True)

        w_qkv, w_out, w_up, w_down, b_up = whole(w_qkv), whole(w_out), whole(w_up), whole(w_down), whole(b_up)
        width = w_out.shape[0]
        extra = columns([whole(vector) for vector in vectors] + list(b_up.reshape(SLICES, width)))
        pairs = [
            (jnp.concatenate([w_qkv[:, :width], extra], 1), jnp.concatenate([w_qkv[:, 2 * width :], extra], 1)),
            (w_qkv[:, width : 2 * width], w_out),
        ]
        for at in range(SLICES):
            here = slice(at * width, (at + 1) * width)
            pairs.append((w_up[:, here], w_down[here]))
        return [tuple(one.reshape(self.blocks, -1, one.shape[1]) for one in pair) for pair in pairs]

    def reduce(self, index, parts):
        return parts.reshape(2, -1, parts.shape[-1]).astype(F32)

    def finish(self, reduced):
        def owned(value):
            return lax.psum_scatter(value, "dp", scatter_dimension=0, tiled=True)

        width = reduced[0].shape[-1]
        small = reduced[1][0][:, width:].T
        up = jnp.concatenate([pair[0] for pair in reduced[2:]], 1)
        down = jnp.concatenate([pair[1] for pair in reduced[2:]], 0)
        qkv = jnp.concatenate([reduced[0][0], reduced[1][0][:, :width], reduced[0][1]], 1)
        vectors = [owned(small[at]) for at in range(8)]
        b_up = owned(small[8 : 8 + SLICES].reshape(-1))
        return vectors, b_up, owned(qkv), owned(reduced[1][1][:, :width]), owned(up), owned(down)


def local(
    tokens, segment, ln1_gain, ln1_bias, w_qkv, b_query, b_value, w_out, b_out, ln2_gain, ln2_bias,
    w_up, b_up, w_down, b_down, cotangent,
):
    plan = Staged() if lax.axis_size("dp") == 32 else Plain()
    vectors = [ln1_gain, ln1_bias, b_query, b_value, b_out, ln2_gain, ln2_bias, b_down]
    weights = plan.gather(vectors, b_up, w_qkv, w_out, w_up, w_down)
    spot = plan.spot
    labels = jnp.array(list(range(RUNS - 1)) + [-1], jnp.int32)
    counts = jnp.sum((segment[None, :] == labels[:, None]).astype(jnp.int32), 1)
    gathered = [plan.gather_order(at) for at in range(SLICES + 2)]
    scattered = [plan.scatter_order(at) for at in range(SLICES + 2)]

    a1t, q, k, v, wq, wk, wv, wo, small = qkv_call(spot, tokens, weights[0], weights[1], gathered[:2])
    mixed, lse = attend_call(counts, q, k, v)
    middle, a2, a2t, mixed_t, gm = out_call(counts, mixed, tokens, wo, small, cotangent)
    result, down = middle, None
    up_sums, reduced = [], [None] * (SLICES + 2)
    for at in range(SLICES):
        orders = (gathered[2 + at], scattered[2 + at])
        result, down, grads, sums = x_feed_call(
            counts, spot, a2, a2t, gm, small, result, down, weights[2 + at], at, orders
        )
        up_sums.append(sums)
        reduced[2 + at] = plan.reduce(2 + at, grads)
    dy, d_mixed, grad_out, mid_sums = x_mid_call(
        counts, spot, middle, down, cotangent, mixed_t, wo, small, plan.blocks, scattered[1]
    )
    dq, dk, dv = attend_back_call(counts, q, k, v, d_mixed, lse)
    grad_tokens, grad_a, grad_b = x_end_call(
        spot, tokens, dy, a1t, dq, dk, dv, wq, wk, wv, small, mid_sums, jnp.concatenate(up_sums, 0), grad_out,
        scattered[:2],
    )
    reduced[0] = plan.reduce(0, grad_a)
    reduced[1] = plan.reduce(1, grad_b)
    vectors, grad_b_up, grad_qkv, grad_w_out, grad_up, grad_down = plan.finish(reduced)
    gain_one, bias_one, grad_query, grad_value, grad_out_bias, gain_two, bias_two, grad_down_bias = vectors
    return (
        result, grad_tokens, gain_one, bias_one, grad_qkv, grad_query, grad_value, grad_w_out, grad_out_bias,
        gain_two, bias_two, grad_up, grad_b_up, grad_down, grad_down_bias,
    )


def solution(mesh):
    matrix, vector = P("dp", None), P("dp")
    return jax.shard_map(
        local,
        mesh=mesh,
        in_specs=(
            matrix, vector, vector, vector, matrix, vector, vector, matrix, vector, vector, vector,
            matrix, vector, matrix, vector, matrix,
        ),
        out_specs=(
            matrix, matrix, vector, vector, matrix, vector, vector, matrix, vector, vector, vector,
            matrix, vector, matrix, vector,
        ),
        check_vma=False,
    )
```

time: 885 us -> 569 us (0.64)
  waiting for transfers between devices: 371 us -> 115 us
  matrix products: 294 us -> 98.5 us
  starting transfers between devices: 0.32 us -> 96.7 us
  local copies, waits for them, and re-layouts: 61.6 us -> 156 us
  blocking collectives: 84.8 us -> 0 us
  Pallas kernels: 0 us -> 35.8 us
  between operations: 14.9 us -> 5.68 us
    reduce_scatter x4 -> x0, waiting for transfers between devices: 287 us -> none  [the longest x1 142 us: local(): lax.psum_scatter(grad_down, 'dp', scatter_dimension=0, tiled=True)]
    dot_general x96 -> x32, matrix products: 294 us -> 98.5 us  [the longest x20 59.3 us: mm(): lax.dot_general(left, right, (((1,), (0,)), ((), ())), preferred_element_...]
    ppermute x0 -> x79, waiting for transfers between devices: none -> 115 us  [flip(): lax.ppermute(value, 'dp', [(at, at ^ bit) for at in range(lax.axis_size('...]
    ppermute x0 -> x79, starting transfers between devices: none -> 96.7 us  [flip(): lax.ppermute(value, 'dp', [(at, at ^ bit) for at in range(lax.axis_size('...]
    unnamed x2 -> x0, blocking collectives: 84.8 us -> none
    all_gather x4 -> x0, waiting for transfers between devices: 81.5 us -> none  [the longest x1 54.6 us: local(): lax.all_gather(shards[11], 'dp', axis=0, tiled=True)]
    gather x0 -> x22, local copies, waits for them, and re-layouts: none -> 60.4 us  [the longest x11 32.6 us: scatter_form(): z, o = (zero.reshape(blocks, -1, W)[src], one.reshape(blocks, -1, W)[src])]
    pallas_call x0 -> x4, Pallas kernels: none -> 35.8 us  [the longest x1 13.6 us: attend_back_call(): pl.pallas_call(functools.partial(attend_back_kernel, scale=(width // HEAD...]
  transfers between devices with their start and end apart: 8 -> 79, of which waited for: 6 -> 31; matrix products, arithmetic and copies ran while one was open for 41% -> 28% of each run, Pallas kernels for 0% -> 0%
where the time goes in v1:
time: 569 us; the launch traced here: 558 us
  local copies, waits for them, and re-layouts  156 us (27%)
  waiting for transfers between devices  115 us (20%)
  matrix products  98.5 us (17%)
  starting transfers between devices  96.7 us (17%)
  other arithmetic  50.4 us (9%)
  Pallas kernels  35.8 us (6%)
    ppermute x79, waiting for transfers between devices, flip(): lax.ppermute(value, 'dp', [(at, at ^ bit) for at in range(lax.axis_size('...  115 us
    ppermute x79, starting transfers between devices, flip(): lax.ppermute(value, 'dp', [(at, at ^ bit) for at in range(lax.axis_size('...  96.7 us
    dot_general x20, matrix products, mm(): lax.dot_general(left, right, (((1,), (0,)), ((), ())), preferred_element_...  59.3 us
    unnamed x217, local copies, waits for them, and re-layouts  40.5 us
    dot_general x12, matrix products, mm_nt(): lax.dot_general(left, right, (((1,), (1,)), ((), ())), preferred_element_...  39.1 us
    gather x11, local copies, waits for them, and re-layouts, scatter_form(): z, o = (zero.reshape(blocks, -1, W)[src], one.reshape(blocks, -1, W)[src])  32.6 us
    gather x8, local copies, waits for them, and re-layouts, assemble(): o, t = (own[pos].reshape(-1, W), oth[pos].reshape(-1, W))  23.4 us
    select_n x5, other arithmetic, scatter_form(): return jnp.where(core == 0, jnp.stack([z, o]), jnp.stack([o, z]))  14.3 us
  transfers between devices with their start and end apart: 79, of which 31 were waited for; matrix products, arithmetic and copies ran while one was open for 28% of the time, Pallas kernels for 0%

profile of v1, /device:TPU:0, one launch (start us, length us, event | category | flops | bytes accessed | tf_op | source)
XLA Modules:
  0.0 558.1 jit_solution(14751587634111869018)
XLA Ops:
  14.8 4.6 slice_reduce_fusion
  52.5 5.7 %collective-permute-done.19 = bf16[48,768]{1,0:T(8,128)(2,1)S(1)} collective-permute-done((bf16[48,768]{1,0:T(8,128)(2,1)S(1)}, bf16[48,768]{1,0:T(8,128)(2,1)S(1)}, u32[]{:S(2)}, u32[]{:S(2)}) %collective-permute-start.19) | collective-permute-done | bytes 73760 | tf_op jit(solution)/shard_map/ppermute | solution.py:636
  59.5 5.1 collective-permute-done.20
  76.2 4.4 collective-permute-done.26
  106.7 7.0 %collective-permute-done.22 = bf16[4,48,768]{2,1,0:T(8,128)(2,1)S(1)} collective-permute-done((bf16[4,48,768]{2,1,0:T(8,128)(2,1)S(1)}, bf16[4,48,768]{2,1,0:T(8,128)(2,1)S(1)}, u32[]{:S(2)}, u32[]{:S(2)}) %collective-permute-start.22) | collective-permute-done | bytes 294944 | tf_op jit(solution)/shard_map/ppermute | solution.py:636
  126.0 6.7 %collective-permute-done.17 = bf16[8,48,768]{2,1,0:T(8,128)(2,1)S(1)} collective-permute-done((bf16[8,48,768]{2,1,0:T(8,128)(2,1)S(1)}, bf16[8,48,768]{2,1,0:T(8,128)(2,1)S(1)}, u32[]{:S(2)}, u32[]{:S(2)}) %collective-permute-start.17) | collective-permute-done | bytes 589856 | tf_op jit(solution)/shard_map/ppermute | solution.py:636
  136.2 7.1 %collective-permute-done.29 = bf16[8,48,768]{2,1,0:T(8,128)(2,1)S(1)} collective-permute-done((bf16[8,48,768]{2,1,0:T(8,128)(2,1)S(1)}, bf16[8,48,768]{2,1,0:T(8,128)(2,1)S(1)}, u32[]{:S(2)}, u32[]{:S(2)}) %collective-permute-start.29) | collective-permute-done | bytes 589856 | tf_op jit(solution)/shard_map/ppermute | solution.py:636
  145.5 6.2 %collective-permute-done.5 = bf16[8,48,1024]{2,1,0:T(8,128)(2,1)S(1)} collective-permute-done((bf16[8,48,1024]{2,1,0:T(8,128)(2,1)S(1)}, bf16[8,48,1024]{2,1,0:T(8,128)(2,1)S(1)}, u32[]{:S(2)}, u32[]{:S(2)}) %collective-permute-start.5) | collective-permute-done | bytes 786464 | tf_op jit(solution)/shard_map/ppermute | solution.py:636
  188.2 8.6 %norm_qkv.1 = (bf16[768,1024]{1,0:T(8,128)(2,1)S(1)}, bf16[1024,768]{1,0:T(8,128)(2,1)S(1)}, bf16[1024,768]{1,0:T(8,128)(2,1)S(1)}, bf16[1024,768]{1,0:T(8,128)(...) custom-call(s32[2]{0:T(128)S(1)} %pad_add_fusion.spot, ...), custom_call_target="tpu_custom_call" | custom-call | flops 3623878656 | bytes 9437184 | tf_op jit(solution)/shard_map/norm_qkv/pallas_call | solution.py:142
  200.7 10.3 %attend.1 = (bf16[1024,768]{1,0:T(8,128)(2,1)S(1)}, f32[14,1,16,384]{3,2,1,0:T(8,128)S(1)}) custom-call(s32[6]{0:T(128)S(1)} %convert_reduce_fusion.1.counts, bf16[1024,768]{1,0:T(8,128)(2,1)S(1)} %get-tuple-element.34.q_ref, bf16[1024,768]{1,0:T(8,128)(2,1)S(1)} %get-tuple-element.35.k_ref, bf16[1024,768]{1,0:T(8,128)(2,1)S(1)} %get-tuple-element.36.v_ref), custom_call_target="tpu_custom_call" | custom-call | flops 1610612736 | bytes 6291456 | tf_op jit(solution)/shard_map/attend/pallas_call | solution.py:247
  247.3 4.1 fusion.97
  261.3 4.3 fusion.95
  270.0 5.6 multiply_reduce_fusion
  281.7 13.6 %attend_back.1 = (bf16[1024,768]{1,0:T(8,128)(2,1)S(1)}, bf16[1024,768]{1,0:T(8,128)(2,1)S(1)}, bf16[1024,768]{1,0:T(8,128)(2,1)S(1)}) custom-call(s32[6]{0:T(128)S(1)} %convert_reduce_fusion.1.counts, bf16[1024,768]{1,0:T(8,128)(2,1)S(1)} %copy-done.18, bf16[1024,768]{1,0:T(8,128)(2,1)S(1)} %copy-done.20, bf16[1024,768]{1,0:T(8,128)(2,1)S(1)} %copy-done.22, ...), custom_call_target="tpu_custom_call" | custom-call | flops 4026531840 | bytes 14155776 | tf_op jit(solution)/shard_map/attend_back/pallas_call | solution.py:316
  302.2 4.4 convolution_convert_fusion.10
  331.8 5.0 collective-permute-start.51
  378.1 4.1 fusion.10
  401.8 4.3 convolution_convert_fusion.11
  423.6 6.7 %add_convert_fusion = bf16[1024,768]{1,0:T(8,128)(2,1)} fusion(f32[1024,768]{1,0:T(8,128)} %fusion.93, f32[1024,768]{1,0:T(8,128)} %fusion.92, f32[1024,768]{1,0:T(8,128)S(1)} %get-tuple-element.40, f32[1024,768]{1,0:T(8,128)} %fusion.91, f32[768]{0:T(1024)S(1)} %copy-done.72, pred[1024]{0:T(1024)(128)(4,1)S(1)} %copy-done.79, ...), kind=kOutput, calls=%fused_computation.82 | convolution fusion | flops 1224474624 | bytes 18488320 | tf_op jit(solution)/shard_map/dot_general | solution.py:41
  456.6 7.3 %collective-permute-done.66 = bf16[8,48,768]{2,1,0:T(8,128)(2,1)S(1)} collective-permute-done((bf16[8,48,768]{2,1,0:T(8,128)(2,1)S(1)}, bf16[8,48,768]{2,1,0:T(8,128)(2,1)S(1)}, u32[]{:S(2)}, u32[]{:S(2)}) %collective-permute-start.66) | collective-permute-done | bytes 589856 | tf_op jit(solution)/shard_map/ppermute | solution.py:636
  469.2 7.3 %collective-permute-done.45 = bf16[8,48,768]{2,1,0:T(8,128)(2,1)S(1)} collective-permute-done((bf16[8,48,768]{2,1,0:T(8,128)(2,1)S(1)}, bf16[8,48,768]{2,1,0:T(8,128)(2,1)S(1)}, u32[]{:S(2)}, u32[]{:S(2)}) %collective-permute-start.45) | collective-permute-done | bytes 589856 | tf_op jit(solution)/shard_map/ppermute | solution.py:636
  478.3 12.1 %collective-permute-done.53 = bf16[4,48,768]{2,1,0:T(8,128)(2,1)S(1)} collective-permute-done((bf16[4,48,768]{2,1,0:T(8,128)(2,1)S(1)}, bf16[4,48,768]{2,1,0:T(8,128)(2,1)S(1)}, u32[]{:S(2)}, u32[]{:S(2)}) %collective-permute-start.53) | collective-permute-done | bytes 294944 | tf_op jit(solution)/shard_map/ppermute | solution.py:636
  492.5 4.2 collective-permute-done.67
  533.8 9.3 %collective-permute-done.39 = bf16[4,48,1024]{2,1,0:T(8,128)(2,1)S(1)} collective-permute-done((bf16[4,48,1024]{2,1,0:T(8,128)(2,1)S(1)}, bf16[4,48,1024]{2,1,0:T(8,128)(2,1)S(1)}, u32[]{:S(2)}, u32[]{:S(2)}) %collective-permute-start.39) | collective-permute-done | bytes 393248 | tf_op jit(solution)/shard_map/ppermute | solution.py:636
  (567 shorter events, 394.5 us)
Async XLA Ops:
  44.3 43.3 %collective-permute-start.9 = (bf16[48,768]{1,0:T(8,128)(2,1)S(1)}, bf16[48,768]{1,0:T(8,128)(2,1)S(1)}, u32[]{:S(2)}, u32[]{:S(2)}) collective-permute-start(bf16[48,768]{1,0:T(8,128)(2,1)S(1)} %get-tuple-element.159), channel_id=1, source_target_pairs={{0,24},{1,25},{2,26},{3,27},{4,28},{5,29},{6,30},{7,31},{8,16},{9,... | collective-permute-start | bytes 221192 | tf_op jit(solution)/shard_map/ppermute | solution.py:636
  45.0 54.8 %collective-permute-start.1 = (bf16[48,1024]{1,0:T(8,128)(2,1)S(1)}, bf16[48,1024]{1,0:T(8,128)(2,1)S(1)}, u32[]{:S(2)}, u32[]{:S(2)}) collective-permute-start(bf16[48,1024]{1,0:T(8,128)(2,1)S(1)} %get-tuple-element.103), channel_id=1, source_target_pairs={{0,8},{1,9},{2,10},{3,11},{4,12},{5,13},{6,14},{7,15},{8,0},{9,1},... | collective-permute-start | bytes 294920 | tf_op jit(solution)/shard_map/ppermute | solution.py:636
  46.2 54.1 %collective-permute-start.2 = (bf16[48,1024]{1,0:T(8,128)(2,1)S(1)}, bf16[48,1024]{1,0:T(8,128)(2,1)S(1)}, u32[]{:S(2)}, u32[]{:S(2)}) collective-permute-start(bf16[48,1024]{1,0:T(8,128)(2,1)S(1)} %get-tuple-element.103), channel_id=1, source_target_pairs={{0,16},{1,17},{2,18},{3,19},{4,20},{5,21},{6,22},{7,23},{8,24},{9,... | collective-permute-start | bytes 294920 | tf_op jit(solution)/shard_map/ppermute | solution.py:636
  50.7 51.3 %collective-permute-start.3 = (bf16[48,1024]{1,0:T(8,128)(2,1)S(1)}, bf16[48,1024]{1,0:T(8,128)(2,1)S(1)}, u32[]{:S(2)}, u32[]{:S(2)}) collective-permute-start(bf16[48,1024]{1,0:T(8,128)(2,1)S(1)} %get-tuple-element.103), channel_id=1, source_target_pairs={{0,24},{1,25},{2,26},{3,27},{4,28},{5,29},{6,30},{7,31},{8,16},{9,... | collective-permute-start | bytes 294920 | tf_op jit(solution)/shard_map/ppermute | solution.py:636
  97.5 26.5 %collective-permute-start.10 = (bf16[4,48,768]{2,1,0:T(8,128)(2,1)S(1)}, bf16[4,48,768]{2,1,0:T(8,128)(2,1)S(1)}, u32[]{:S(2)}, u32[]{:S(2)}) collective-permute-start(bf16[4,48,768]{2,1,0:T(8,128)(2,1)S(1)} %pad_maximum_fusion.2), channel_id=1, source_target_pairs={{0,4},{1,5},{2,6},{3,7},{4,0},{5,1},{6,2},{7,3},{8,12},{9,13},{10,... | collective-permute-start | bytes 884744 | tf_op jit(solution)/shard_map/ppermute | solution.py:636
  120.0 23.3 %collective-permute-start.29 = (bf16[8,48,768]{2,1,0:T(8,128)(2,1)S(1)}, bf16[8,48,768]{2,1,0:T(8,128)(2,1)S(1)}, u32[]{:S(2)}, u32[]{:S(2)}) collective-permute-start(bf16[8,48,768]{2,1,0:T(8,128)(2,1)S(1)} %get-tuple-element.176), channel_id=1, source_target_pairs={{0,4},{1,5},{2,6},{3,7},{4,0},{5,1},{6,2},{7,3},{8,12},{9,13},{10,... | collective-permute-start | bytes 1769480 | tf_op jit(solution)/shard_map/ppermute | solution.py:636
  124.0 27.7 %collective-permute-start.5 = (bf16[8,48,1024]{2,1,0:T(8,128)(2,1)S(1)}, bf16[8,48,1024]{2,1,0:T(8,128)(2,1)S(1)}, u32[]{:S(2)}, u32[]{:S(2)}) collective-permute-start(bf16[8,48,1024]{2,1,0:T(8,128)(2,1)S(1)} %get-tuple-element.166), channel_id=1, source_target_pairs={{0,4},{1,5},{2,6},{3,7},{4,0},{5,1},{6,2},{7,3},{8,12},{9,13},{10,... | collective-permute-start | bytes 2359304 | tf_op jit(solution)/shard_map/ppermute | solution.py:636
  135.1 33.0 %collective-permute-start.18 = (bf16[16,48,768]{2,1,0:T(8,128)(2,1)}, bf16[16,48,768]{2,1,0:T(8,128)(2,1)}, u32[]{:S(2)}, u32[]{:S(2)}) collective-permute-start(bf16[16,48,768]{2,1,0:T(8,128)(2,1)} %constant_dynamic-update-slice_fusion.41), channel_id=1, source_target_pairs={{0,1},{1,0},{2,3},{3,2},{4,5},{5,4},{6,7},{7,6},{8,9},{9,8},{10,11... | collective-permute-start | bytes 3538952 | tf_op jit(solution)/shard_map/ppermute | solution.py:636
  143.3 31.5 %collective-permute-start.24 = (bf16[16,48,768]{2,1,0:T(8,128)(2,1)}, bf16[16,48,768]{2,1,0:T(8,128)(2,1)}, u32[]{:S(2)}, u32[]{:S(2)}) collective-permute-start(bf16[16,48,768]{2,1,0:T(8,128)(2,1)} %constant_dynamic-update-slice_fusion.52), channel_id=1, source_target_pairs={{0,1},{1,0},{2,3},{3,2},{4,5},{5,4},{6,7},{7,6},{8,9},{9,8},{10,11... | collective-permute-start | bytes 3538952 | tf_op jit(solution)/shard_map/ppermute | solution.py:636
  144.2 33.6 %collective-permute-start.30 = (bf16[16,48,768]{2,1,0:T(8,128)(2,1)}, bf16[16,48,768]{2,1,0:T(8,128)(2,1)}, u32[]{:S(2)}, u32[]{:S(2)}) collective-permute-start(bf16[16,48,768]{2,1,0:T(8,128)(2,1)} %constant_dynamic-update-slice_fusion.63), channel_id=1, source_target_pairs={{0,1},{1,0},{2,3},{3,2},{4,5},{5,4},{6,7},{7,6},{8,9},{9,8},{10,11... | collective-permute-start | bytes 3538952 | tf_op jit(solution)/shard_map/ppermute | solution.py:636
  151.7 28.9 %collective-permute-start.36 = (bf16[16,48,768]{2,1,0:T(8,128)(2,1)}, bf16[16,48,768]{2,1,0:T(8,128)(2,1)}, u32[]{:S(2)}, u32[]{:S(2)}) collective-permute-start(bf16[16,48,768]{2,1,0:T(8,128)(2,1)} %constant_dynamic-update-slice_fusion.74), channel_id=1, source_target_pairs={{0,1},{1,0},{2,3},{3,2},{4,5},{5,4},{6,7},{7,6},{8,9},{9,8},{10,11... | collective-permute-start | bytes 3538952 | tf_op jit(solution)/shard_map/ppermute | solution.py:636
  153.7 34.5 %collective-permute-start.6 = (bf16[16,48,1024]{2,1,0:T(8,128)(2,1)S(1)}, bf16[16,48,1024]{2,1,0:T(8,128)(2,1)}, u32[]{:S(2)}, u32[]{:S(2)}) collective-permute-start(bf16[16,48,1024]{2,1,0:T(8,128)(2,1)S(1)} %constant_dynamic-update-slice_fusion.19.ta0), channel_id=1, source_target_pairs={{0,1},{1,0},{2,3},{3,2},{4,5},{5,4},{6,7},{7,6},{8,9},{9,8},{10,11... | collective-permute-start | bytes 4718600 | tf_op jit(solution)/shard_map/ppermute | solution.py:636
  331.8 98.5 %collective-permute-start.51 = (bf16[16,48,768]{2,1,0:T(8,128)(2,1)}, bf16[16,48,768]{2,1,0:T(8,128)(2,1)}, u32[]{:S(2)}, u32[]{:S(2)}) collective-permute-start(bf16[16,48,768]{2,1,0:T(8,128)(2,1)} %slice_bitcast_fusion.4), channel_id=1, source_target_pairs={{0,1},{1,0},{2,3},{3,2},{4,5},{5,4},{6,7},{7,6},{8,9},{9,8},{10,11... | collective-permute-start | bytes 3538952 | tf_op jit(solution)/shard_map/ppermute | solution.py:636
  348.0 87.0 %collective-permute-start.58 = (bf16[16,48,768]{2,1,0:T(8,128)(2,1)}, bf16[16,48,768]{2,1,0:T(8,128)(2,1)}, u32[]{:S(2)}, u32[]{:S(2)}) collective-permute-start(bf16[16,48,768]{2,1,0:T(8,128)(2,1)} %slice_bitcast_fusion.3), channel_id=1, source_target_pairs={{0,1},{1,0},{2,3},{3,2},{4,5},{5,4},{6,7},{7,6},{8,9},{9,8},{10,11... | collective-permute-start | bytes 3538952 | tf_op jit(solution)/shard_map/ppermute | solution.py:636
  359.3 78.9 %collective-permute-start.65 = (bf16[16,48,768]{2,1,0:T(8,128)(2,1)}, bf16[16,48,768]{2,1,0:T(8,128)(2,1)}, u32[]{:S(2)}, u32[]{:S(2)}) collective-permute-start(bf16[16,48,768]{2,1,0:T(8,128)(2,1)} %slice_bitcast_fusion.2), channel_id=1, source_target_pairs={{0,1},{1,0},{2,3},{3,2},{4,5},{5,4},{6,7},{7,6},{8,9},{9,8},{10,11... | collective-permute-start | bytes 3538952 | tf_op jit(solution)/shard_map/ppermute | solution.py:636
  369.7 72.0 %collective-permute-start.72 = (bf16[16,48,768]{2,1,0:T(8,128)(2,1)}, bf16[16,48,768]{2,1,0:T(8,128)(2,1)}, u32[]{:S(2)}, u32[]{:S(2)}) collective-permute-start(bf16[16,48,768]{2,1,0:T(8,128)(2,1)} %slice_bitcast_fusion.1), channel_id=1, source_target_pairs={{0,1},{1,0},{2,3},{3,2},{4,5},{5,4},{6,7},{7,6},{8,9},{9,8},{10,11... | collective-permute-start | bytes 3538952 | tf_op jit(solution)/shard_map/ppermute | solution.py:636
  413.5 31.2 %collective-permute-start.37 = (bf16[16,48,1024]{2,1,0:T(8,128)(2,1)}, bf16[16,48,1024]{2,1,0:T(8,128)(2,1)}, u32[]{:S(2)}, u32[]{:S(2)}) collective-permute-start(bf16[16,48,1024]{2,1,0:T(8,128)(2,1)} %slice_bitcast_fusion), channel_id=1, source_target_pairs={{0,1},{1,0},{2,3},{3,2},{4,5},{5,4},{6,7},{7,6},{8,9},{9,8},{10,11... | collective-permute-start | bytes 4718600 | tf_op jit(solution)/shard_map/ppermute | solution.py:636
  444.1 23.1 %collective-permute-start.73 = (bf16[8,48,768]{2,1,0:T(8,128)(2,1)S(1)}, bf16[8,48,768]{2,1,0:T(8,128)(2,1)S(1)}, u32[]{:S(2)}, u32[]{:S(2)}) collective-permute-start(bf16[8,48,768]{2,1,0:T(8,128)(2,1)S(1)} %get-tuple-element.115), channel_id=1, source_target_pairs={{0,4},{1,5},{2,6},{3,7},{4,0},{5,1},{6,2},{7,3},{8,12},{9,13},{10,... | collective-permute-start | bytes 1769480 | tf_op jit(solution)/shard_map/ppermute | solution.py:636
  444.7 31.9 %collective-permute-start.45 = (bf16[8,48,768]{2,1,0:T(8,128)(2,1)S(1)}, bf16[8,48,768]{2,1,0:T(8,128)(2,1)S(1)}, u32[]{:S(2)}, u32[]{:S(2)}) collective-permute-start(bf16[8,48,768]{2,1,0:T(8,128)(2,1)S(1)} %get-tuple-element.117), channel_id=1, source_target_pairs={{0,2},{1,3},{2,0},{3,1},{4,6},{5,7},{6,4},{7,5},{8,10},{9,11},{10,... | collective-permute-start | bytes 1769480 | tf_op jit(solution)/shard_map/ppermute | solution.py:636
  451.2 80.4 %collective-permute-start.38 = (bf16[8,48,1024]{2,1,0:T(8,128)(2,1)S(1)}, bf16[8,48,1024]{2,1,0:T(8,128)(2,1)S(1)}, u32[]{:S(2)}, u32[]{:S(2)}) collective-permute-start(bf16[8,48,1024]{2,1,0:T(8,128)(2,1)S(1)} %get-tuple-element.107), channel_id=1, source_target_pairs={{0,4},{1,5},{2,6},{3,7},{4,0},{5,1},{6,2},{7,3},{8,12},{9,13},{10,... | collective-permute-start | bytes 2359304 | tf_op jit(solution)/shard_map/ppermute | solution.py:636
  454.5 35.8 %collective-permute-start.53 = (bf16[4,48,768]{2,1,0:T(8,128)(2,1)S(1)}, bf16[4,48,768]{2,1,0:T(8,128)(2,1)S(1)}, u32[]{:S(2)}, u32[]{:S(2)}) collective-permute-start(bf16[4,48,768]{2,1,0:T(8,128)(2,1)S(1)} %get-tuple-element.129), channel_id=1, source_target_pairs={{0,4},{1,5},{2,6},{3,7},{4,0},{5,1},{6,2},{7,3},{8,12},{9,13},{10,... | collective-permute-start | bytes 884744 | tf_op jit(solution)/shard_map/ppermute | solution.py:636
  463.9 28.4 %collective-permute-start.60 = (bf16[4,48,768]{2,1,0:T(8,128)(2,1)S(1)}, bf16[4,48,768]{2,1,0:T(8,128)(2,1)S(1)}, u32[]{:S(2)}, u32[]{:S(2)}) collective-permute-start(bf16[4,48,768]{2,1,0:T(8,128)(2,1)S(1)} %get-tuple-element.131), channel_id=1, source_target_pairs={{0,2},{1,3},{2,0},{3,1},{4,6},{5,7},{6,4},{7,5},{8,10},{9,11},{10,... | collective-permute-start | bytes 884744 | tf_op jit(solution)/shard_map/ppermute | solution.py:636
  467.2 29.5 %collective-permute-start.67 = (bf16[4,48,768]{2,1,0:T(8,128)(2,1)S(1)}, bf16[4,48,768]{2,1,0:T(8,128)(2,1)S(1)}, u32[]{:S(2)}, u32[]{:S(2)}) collective-permute-start(bf16[4,48,768]{2,1,0:T(8,128)(2,1)S(1)} %get-tuple-element.133), channel_id=1, source_target_pairs={{0,4},{1,5},{2,6},{3,7},{4,0},{5,1},{6,2},{7,3},{8,12},{9,13},{10,... | collective-permute-start | bytes 884744 | tf_op jit(solution)/shard_map/ppermute | solution.py:636
  476.5 22.2 %collective-permute-start.74 = (bf16[4,48,768]{2,1,0:T(8,128)(2,1)S(1)}, bf16[4,48,768]{2,1,0:T(8,128)(2,1)S(1)}, u32[]{:S(2)}, u32[]{:S(2)}) collective-permute-start(bf16[4,48,768]{2,1,0:T(8,128)(2,1)S(1)} %get-tuple-element.135), channel_id=1, source_target_pairs={{0,2},{1,3},{2,0},{3,1},{4,6},{5,7},{6,4},{7,5},{8,10},{9,11},{10,... | collective-permute-start | bytes 884744 | tf_op jit(solution)/shard_map/ppermute | solution.py:636
  (146 other events, 1752.1 us)
